TPU v7x, 32 devices: a whole 2x2x4 slice. The times are simulated.
32 devices in a mesh: runs: 2 (over x), gy: 16 (over z, y, core).
Axes of the slice: x: 2, y: 2, z: 4, core: 2. Of those that a mesh axis runs over, the one named last changes fastest.
Arguments:
- depth: float32 [1024, 1920], P(('runs', 'gy')), parts along dimension 0, may hold values from 0.02 to 3
- flux_east: float32 [1024, 1920], P(('runs', 'gy')), parts along dimension 0, may hold values from -2 to 2
- flux_south: float32 [1024, 1920], P(('runs', 'gy')), parts along dimension 0, may hold values from -2 to 2
- river_section: float32 [4096], P(('runs', 'gy')), parts along dimension 0, may hold values from 0 to 2
- bed_level: float32 [512, 1920], P('gy'), may hold values from -3 to 3
- rough_class: int32 [512, 1920], P('gy'), may hold values from 0 to 7
- manning_table: float32 [8], replicated, may hold values from 0.02 to 0.15
- bank_cell: int32 [4, 2048], P(None, 'gy'), may hold values from 0 to 983039, as said below
Outputs:
- depth_out: float32 [1024, 1920], P(('runs', 'gy')), parts along dimension 0
- east_out: float32 [1024, 1920], P(('runs', 'gy')), parts along dimension 0
- south_out: float32 [1024, 1920], P(('runs', 'gy')), parts along dimension 0
- section_out: float32 [4096], P(('runs', 'gy')), parts along dimension 0
There are 2 independent parts, one for each index of `runs`. A program takes and returns all parts, laid end to end along the dimension named above; an argument that names none is the same for every part. Nothing has to cross between parts.
Inputs may be any that keep to these rules, and one draw needn't show every extreme that they name: `bank_cell`: the 4 corridor cells of a node are consecutive flat indices row * 1920 + column within one map row. Node n is owned by gy index o = n // 128, and all its corridor cells lie in map rows from max((o - 1) * 32, 0) to min((o + 2) * 32, 512) - 1.
All inputs are finite; a program needn't handle non-finite values.
Results may differ from a plain program's by a relative error of at most 0.00013.
Values sent between devices are 32-bit elements; how exact they have to be, the bound alone decides.
A program may use at most 64 MiB of HBM per device.

v0:
```python
import math

import jax
import jax.numpy as jnp
from jax import lax
from jax.experimental import pallas as pl
from jax.experimental.pallas import tpu as pltpu
from jax.sharding import PartitionSpec as P

STEPS = 4
HALO = STEPS
LANES = 128
TILE = 8

GRAV = 9.81
TSTEP = 8.0
CELL = 90.0
FLOOR = 0.05
BANK_COEF = 200.0
CELL_AREA = 8100.0
NODE_AREA = 20000.0

SLOPE = GRAV * TSTEP / CELL
LEVEL = SLOPE * TSTEP / CELL
FLOW = LEVEL * TSTEP / CELL
ROUGH = math.sqrt(0.25 * GRAV * TSTEP * LEVEL ** (7.0 / 3.0) / FLOW)
KEEP = 1.0 - TSTEP * BANK_COEF * 4.0 / NODE_AREA
GAIN = TSTEP * BANK_COEF / NODE_AREA
INTO = TSTEP * BANK_COEF / CELL_AREA

MESH = pl.DeviceIdType.MESH
VMEM_BYTES = 24 * 1024 * 1024
FAR = -(1 << 24)
OFFSETS = (-1, 1, -2, 2)


def wave(batches):
    running, waiting = [], list(batches)
    while running or waiting:
        if waiting:
            running.extend(waiting.pop(0))
        for unit in list(running):
            try:
                next(unit)
            except StopIteration:
                running.remove(unit)


def by(size, units):
    units = list(units)
    return [units[i : i + size] for i in range(0, len(units), size)]


def halves(value):
    high = value.astype(jnp.bfloat16)
    return high, (value - high.astype(jnp.float32)).astype(jnp.bfloat16)


def flood_kernel(
    table_in,
    depth_in,
    east_in,
    south_in,
    bed_in,
    rough_in,
    section_in,
    cells_in,
    depth_out,
    east_out,
    south_out,
    section_out,
    table,
    raw,
    raw_rough,
    edge,
    edge_rough,
    surf,
    fe,
    fs,
    bed,
    mann,
    max_e,
    max_s,
    drag_e,
    drag_s,
    tally,
    number,
    number4,
    boxes,
    partial,
    sections,
    cells,
    part,
    low,
    high,
    in_sem,
    strip_ssem,
    strip_rsem,
    node_ssem,
    node_rsem,
    part_ssem,
    part_rsem,
):
    me = lax.axis_index("gy")
    tiles = lax.axis_size("gy")
    rows, columns = depth_in.shape
    ext = rows + 2 * HALO
    chunks = columns // LANES
    owned = section_in.shape[1]
    total = 5 * owned

    def there(offset):
        return (me + offset >= 0) & (me + offset < tiles)

    def absent(offset):
        return jnp.logical_not(there(offset))

    barrier = pltpu.get_barrier_semaphore()
    for offset in OFFSETS:
        @pl.when(there(offset))
        def _():
            pl.semaphore_signal(
                barrier, inc=1, device_id={"gy": me + offset}, device_id_type=MESH
            )

    fields = (depth_in, bed_in, east_in, south_in)
    loads = [
        pltpu.make_async_copy(source, target, in_sem.at[i])
        for i, (source, target) in enumerate(
            [(field, raw.at[i]) for i, field in enumerate(fields)]
            + [
                (rough_in, raw_rough),
                (table_in, table),
                (section_in, sections.at[2]),
                (cells_in, cells.at[2]),
            ]
        )
    ]
    for load in loads:
        load.start()

    def send(src, dst, ssem, rsem, offset):
        return pltpu.make_async_remote_copy(
            src_ref=src,
            dst_ref=dst,
            send_sem=ssem,
            recv_sem=rsem,
            device_id={"gy": me + offset},
            device_id_type=MESH,
        )

    node_sends = {}
    for i, offset in enumerate(OFFSETS):
        slot = 2 - offset
        node_sends[offset] = (
            send(section_in, sections.at[slot], node_ssem.at[0, i], node_rsem.at[0, i], offset),
            send(cells_in, cells.at[slot], node_ssem.at[1, i], node_rsem.at[1, i], offset),
        )
    strip_sends = {}
    for i, offset in enumerate((-1, 1)):
        theirs = slice(0, HALO) if offset < 0 else slice(rows - HALO, rows)
        lands = slice(0, HALO) if offset < 0 else slice(HALO, 2 * HALO)
        sources = [field.at[theirs] for field in fields] + [rough_in.at[theirs]]
        targets = [edge.at[j, lands] for j in range(4)] + [edge_rough.at[lands]]
        strip_sends[offset] = [
            send(source, target, strip_ssem.at[i, j], strip_rsem.at[i, j], offset)
            for j, (source, target) in enumerate(zip(sources, targets))
        ]

    pl.semaphore_wait(barrier, jnp.minimum(me, 2) + jnp.minimum(tiles - 1 - me, 2))
    for offset in OFFSETS:
        @pl.when(there(offset))
        def _():
            for copy in node_sends[offset]:
                copy.start()

    for offset in (-1, 1):
        @pl.when(there(offset))
        def _():
            for copy in strip_sends[offset]:
                copy.start()

    for load in loads:
        load.wait()

    scaled = [table[k] * ROUGH for k in range(table.shape[0])]

    def roughness(rough):
        values, bit = scaled, 1
        while len(values) > 1:
            odd = (rough & bit) != 0
            values = [
                jnp.where(odd, values[i + 1], values[i]) if i + 1 < len(values) else values[i]
                for i in range(0, len(values), 2)
            ]
            bit *= 2
        return values[0]

    def at(c):
        return slice(LANES * c, LANES * (c + 1))

    lane_id = lax.broadcasted_iota(jnp.int32, (1, LANES), 1)

    def turn(value, shift):
        return pltpu.roll(value, LANES - shift, 1)

    def lanes_to(value, preceding, shift):
        mixed = jnp.where(lane_id >= LANES - shift, preceding, value)
        return pltpu.roll(mixed, shift, 1)

    def south(value):
        return pltpu.roll(value, value.shape[0] - 1, 0)

    def north(value):
        return pltpu.roll(value, 1, 0)

    row_id = lax.broadcasted_iota(jnp.int32, (TILE, LANES), 0)
    shut_last = (row_id == TILE - 1) & (me == tiles - 1)
    shut_first = (row_id == TILE - 1) & (me == 0)

    def depth_of(surf_a, surf_b, bed_top):
        return jnp.maximum(jnp.maximum(surf_a, surf_b) - bed_top, FLOOR * LEVEL)

    def power_log(flow_depth):
        return jnp.log(flow_depth) * (-7.0 / 3.0)

    def damping(flux, drag, power):
        return 1.0 / (1.0 + drag * jnp.abs(flux) * power)

    def square(value):
        return value * value

    def closed_east(c, flux):
        return jnp.where(lane_id == LANES - 1, 0.0, flux) if c == chunks - 1 else flux

    def closed_south(flux):
        count = flux.shape[0]
        return jnp.concatenate(
            [flux[: count - 2 * TILE]] * (count > 2 * TILE)
            + [
                jnp.where(shut_last, 0.0, flux[count - 2 * TILE : count - TILE]),
                jnp.where(shut_first, 0.0, flux[count - TILE :]),
            ],
            axis=0,
        )

    def last_four(value, carried):
        pair = value + lanes_to(value, carried[0], 1)
        return pair + lanes_to(pair, carried[1], 2), (value, pair)

    def zeros(count):
        return jnp.zeros((count, LANES), jnp.float32)

    after = {}

    def put(name, c, value):
        after[name, c] = value

    def got(name, c, count):
        return after.get((name, c), zeros(count))

    inner = rows - TILE

    def own_chunk(c):
        floor = raw[1, :, at(c)] * LEVEL
        bed[:rows, at(c)] = floor
        mine = roughness(raw_rough[:, at(c)])
        mann[:rows, at(c)] = mine
        here = raw[0, :, at(c)] * LEVEL + floor
        surf[:rows, at(c)] = here
        turned = [turn(a, 1) for a in (here, floor, mine)]
        put("own", c, (here, turned))
        yield
        yield
        following = after.get(("own", c + 1), (zeros(rows), [zeros(rows)] * 3))
        east, floor_e, mann_e = (
            jnp.where(lane_id < LANES - 1, a, b) for a, b in zip(turned, following[1])
        )
        pair = here + east
        pair_next = following[0] + following[1][0]
        mixed = turn(jnp.where(lane_id < 2, pair_next, pair), 2)
        top = jnp.maximum(floor, floor_e)
        drag = square(mine + mann_e)
        max_e[:rows, at(c)] = top
        drag_e[:rows, at(c)] = drag
        depth_e = depth_of(here, east, top)
        log_e = power_log(depth_e)
        below_s = south(here)[:inner]
        top = jnp.maximum(floor, south(floor))[:inner]
        drag_b = square((mine + south(mine))[:inner])
        max_s[:inner, at(c)] = top
        drag_s[:inner, at(c)] = drag_b
        depth_s = depth_of(here[:inner], below_s, top)
        log_s = power_log(depth_s)
        yield
        boxes[:rows, at(c)] = pair + mixed
        power_e, power_s = jnp.exp(log_e), jnp.exp(log_s)
        flux_e = raw[2, :, at(c)] * FLOW
        flux_s = raw[3, :inner, at(c)] * FLOW
        yield
        damp_e = damping(flux_e, drag, power_e)
        damp_s = damping(flux_s, drag_b, power_s)
        yield
        new_east = closed_east(c, (flux_e - depth_e * (east - here)) * damp_e)
        new_south = (flux_s - depth_s * (below_s - here[:inner])) * damp_s
        fe[:rows, at(c)] = new_east
        fs[:inner, at(c)] = new_south
        put("east", c, new_east)
        west = lanes_to(new_east, got("east", c - 1, rows), 1)
        yield
        partial[:, at(c)] = here + (west - new_east)

    wave(by(1, (own_chunk(c) for c in range(chunks))))
    after.clear()

    for offset in OFFSETS:
        @pl.when(there(-offset))
        def _():
            for copy in node_sends[offset]:
                copy.wait_recv()

        @pl.when(absent(-offset))
        def _():
            sections[2 - offset] = jnp.zeros((1, owned), jnp.float32)
            cells[2 - offset] = jnp.full((cells.shape[1], owned), FAR, jnp.int32)

    section = jnp.concatenate([sections[i] for i in range(5)], axis=1)
    cell = jnp.concatenate([cells[i, 0:1, :] for i in range(5)], axis=1)
    local = cell - (me * rows - HALO) * columns
    valid = (local >= 0) & (local < ext * columns)
    local = jnp.where(valid, local, 0)
    from_top = ((local.astype(jnp.float32) + 0.5) * (1.0 / columns)).astype(jnp.int32)
    column = local - from_top * columns
    chunk = column >> 7
    lane = column & (LANES - 1)
    own = valid & (from_top >= HALO) & (from_top < rows + HALO)
    place = jnp.where(own, chunk * rows + from_top - HALO, -1)
    near = slice(owned, 4 * owned)
    beyond = jnp.where(from_top < HALO, from_top + HALO, from_top - rows - HALO)
    place_edge = jnp.where(valid & jnp.logical_not(own), chunk * TILE + beyond, -1)

    def one_hot(count, index):
        hit = lax.broadcasted_iota(jnp.int32, (count, index.shape[1]), 0) == index
        return jnp.where(hit, 1.0, 0.0).astype(jnp.bfloat16)

    hit = one_hot(chunks * rows, place[:, near])
    hit_edge = one_hot(-(-chunks * TILE // 16) * 16, place_edge)
    lane_hit = lax.broadcasted_iota(jnp.int32, (LANES, total), 0) == lane
    levels = section * (LEVEL * INTO)
    level_high = levels.astype(jnp.bfloat16).astype(jnp.float32)
    weights = jnp.concatenate(
        [
            jnp.where(lane_hit, value, 0.0)
            for value in (level_high, levels - level_high, jnp.ones_like(levels))
        ],
        axis=0,
    ).astype(jnp.bfloat16)
    contract = (((1,), (1,)), ((), ()))
    spread = lax.dot_general(
        hit, weights[:, near], contract, preferred_element_type=jnp.float32
    )
    spread_edge = lax.dot_general(
        hit_edge, weights, contract, preferred_element_type=jnp.float32
    )
    summed = counted = (zeros(ext),) * 2
    for c in range(chunks):
        block = jnp.concatenate(
            [
                spread[c * rows : (c + 1) * rows],
                spread_edge[c * TILE : (c + 1) * TILE],
            ],
            axis=0,
        )
        level = block[:, :LANES] + block[:, LANES : 2 * LANES]
        tally[:, at(c)], summed = last_four(level, summed)
        count = block[:, 2 * LANES :] * INTO
        number4[:, at(c)], counted = last_four(count, counted)
        number[:, at(c)] = count * GAIN

    for i, offset in enumerate((-1, 1)):
        @pl.when(there(-offset))
        def _():
            for copy in strip_sends[offset]:
                copy.wait_recv()

        @pl.when(absent(-offset))
        def _():
            lands = slice(HALO * i, HALO * (i + 1))
            edge[:, lands, :] = jnp.zeros((4, HALO, columns), jnp.float32)
            edge_rough[lands, :] = jnp.zeros((HALO, columns), jnp.int32)

    outer = slice(rows, ext)

    def edge_chunk(c):
        floor = edge[1, :, at(c)] * LEVEL
        here = edge[0, :, at(c)] * LEVEL + floor
        mine = roughness(edge_rough[:, at(c)])
        turned = [turn(a, 1) for a in (here, floor, mine)]
        put("edge", c, (here, turned))
        yield
        yield
        following = after.get(("edge", c + 1), (zeros(TILE), [zeros(TILE)] * 3))
        east, floor_e, mann_e = (
            jnp.where(lane_id < LANES - 1, a, b) for a, b in zip(turned, following[1])
        )
        pair = here + east
        pair_next = following[0] + following[1][0]
        mixed = turn(jnp.where(lane_id < 2, pair_next, pair), 2)
        top = jnp.maximum(floor, floor_e)
        drag = square(mine + mann_e)
        max_e[outer, at(c)] = top
        drag_e[outer, at(c)] = drag
        depth_e = depth_of(here, east, top)
        log_e = power_log(depth_e)
        whole = jnp.concatenate([surf[:rows, at(c)], here], axis=0)
        below_s = south(whole)[inner:]
        floor = jnp.concatenate([bed[:rows, at(c)], floor], axis=0)
        mine = jnp.concatenate([mann[:rows, at(c)], mine], axis=0)
        top = jnp.maximum(floor, south(floor))[inner:]
        drag_b = square((mine + south(mine))[inner:])
        max_s[inner:, at(c)] = top
        drag_s[inner:, at(c)] = drag_b
        depth_s = depth_of(whole[inner:], below_s, top)
        log_s = power_log(depth_s)
        yield
        boxes[outer, at(c)] = pair + mixed
        power_e, power_s = jnp.exp(log_e), jnp.exp(log_s)
        flux_e = edge[2, :, at(c)] * FLOW
        flux_s = jnp.concatenate([raw[3, inner:, at(c)], edge[3, :, at(c)]], axis=0) * FLOW
        yield
        damp_e = damping(flux_e, drag, power_e)
        damp_s = damping(flux_s, drag_b, power_s)
        yield
        new_east = closed_east(c, (flux_e - depth_e * (east - here)) * damp_e)
        new_south = closed_south((flux_s - depth_s * (below_s - whole[inner:])) * damp_s)
        fe[outer, at(c)] = new_east
        fs[inner:, at(c)] = new_south
        put("edge_east", c, new_east)
        west = lanes_to(new_east, got("edge_east", c - 1, TILE), 1)
        new_south = jnp.concatenate([fs[:inner, at(c)], new_south], axis=0)
        yield
        surf[:, at(c)] = (
            jnp.concatenate([partial[:, at(c)], here + (west - new_east)], axis=0)
            + (north(new_south) - new_south)
            + (tally[:, at(c)] - number4[:, at(c)] * whole)
        )

    def chunk_step(step, c):
        last = step == STEPS - 1
        count = rows if last else ext
        span = slice(0, count)
        whole = surf[:, at(c)]
        here = whole[:count]
        turned = turn(here, 1)
        put(("here", step), c, (here, turned))
        yield
        yield
        following = after.get((("here", step), c + 1), (zeros(count), zeros(count)))
        east = jnp.where(lane_id < LANES - 1, turned, following[1])
        depth_e = depth_of(here, east, max_e[span, at(c)])
        log_e = power_log(depth_e)
        below_s = south(whole)
        depth_s = depth_of(whole, below_s, max_s[:, at(c)])
        log_s = power_log(depth_s)
        if not last:
            pair = here + east
            pair_next = following[0] + following[1]
            mixed = turn(jnp.where(lane_id < 2, pair_next, pair), 2)
        box = boxes[span, at(c)]
        moved = number[span, at(c)] * box
        put(("moved", step), c, moved)
        spill = lanes_to(moved, got(("moved", step), c - 1, count), 1)
        yield
        power_e, power_s = jnp.exp(log_e), jnp.exp(log_s)
        if not last:
            boxes[:, at(c)] = KEEP * box + (pair + mixed)
        spill = moved + spill
        put(("spill", step), c, spill)
        spill2 = lanes_to(spill, got(("spill", step), c - 1, count), 2)
        yield
        flux_e, flux_s = fe[span, at(c)], fs[:, at(c)]
        damp_e = damping(flux_e, drag_e[span, at(c)], power_e)
        damp_s = damping(flux_s, drag_s[:, at(c)], power_s)
        source = KEEP**step * tally[span, at(c)] + (spill + spill2) - number4[span, at(c)] * here
        yield
        new_east = closed_east(c, (flux_e - depth_e * (east - here)) * damp_e)
        new_south = closed_south((flux_s - depth_s * (below_s - whole)) * damp_s)
        put(("east", step), c, new_east)
        west = lanes_to(new_east, got(("east", step), c - 1, count), 1)
        if last:
            east_out[:, at(c)] = new_east * (1.0 / FLOW)
            south_out[:, at(c)] = new_south[:rows] * (1.0 / FLOW)
        else:
            fe[:, at(c)] = new_east
            fs[:, at(c)] = new_south
        yield
        level = here + (west - new_east) + (north(new_south) - new_south)[:count] + source
        if last:
            depth_out[:, at(c)] = level * (1.0 / LEVEL) - raw[1, :, at(c)]
        else:
            surf[:, at(c)] = level

    flat = {}

    def node_chunk(c):
        here = surf[:rows, at(c)]
        turned = turn(here, 1)
        put("node", c, (here, turned))
        yield
        yield
        following = after.get(("node", c + 1), (zeros(rows), zeros(rows)))
        pair = here + jnp.where(lane_id < LANES - 1, turned, following[1])
        pair_next = following[0] + following[1]
        mixed = turn(jnp.where(lane_id < 2, pair_next, pair), 2)
        yield
        flat[c] = KEEP * boxes[:rows, at(c)] + (pair + mixed)

    batches = by(3, (edge_chunk(c) for c in range(chunks))) + [[]]
    for step in range(1, STEPS - 1):
        batches += by(1, (chunk_step(step, c) for c in range(chunks)))
    wave(batches + [[]] * 5 + by(3, (node_chunk(c) for c in range(chunks))))
    flat = [flat[c] for c in range(chunks)]

    turned = jnp.concatenate(halves(jnp.concatenate(flat, axis=0).T), axis=0)
    picked = jnp.dot(turned, hit, preferred_element_type=jnp.float32)
    picked = picked[:LANES] + picked[LANES:]
    picked = jnp.sum(jnp.where(lane_hit[:, near], picked, 0.0), axis=0, keepdims=True)
    final = jnp.where(
        own[:, near], KEEP**STEPS * section[:, near] + (GAIN / LEVEL) * picked, 0.0
    )
    for i in range(3):
        part[i] = final[:, i * owned : (i + 1) * owned]

    part_prev = send(part.at[0], high, part_ssem.at[0], part_rsem.at[0], -1)
    part_next = send(part.at[2], low, part_ssem.at[1], part_rsem.at[1], 1)

    @pl.when(there(-1))
    def _():
        part_prev.start()

    @pl.when(there(1))
    def _():
        part_next.start()

    wave(by(1, (chunk_step(STEPS - 1, c) for c in range(chunks))))

    for offset in OFFSETS:
        @pl.when(there(offset))
        def _():
            for copy in node_sends[offset]:
                copy.wait_send()

    for offset in (-1, 1):
        @pl.when(there(offset))
        def _():
            for copy in strip_sends[offset]:
                copy.wait_send()

    section_out[...] = part[1]

    @pl.when(there(1))
    def _():
        part_prev.wait_recv()
        section_out[...] += high[...]

    @pl.when(there(-1))
    def _():
        part_next.wait_recv()
        section_out[...] += low[...]

    @pl.when(there(-1))
    def _():
        part_prev.wait_send()

    @pl.when(there(1))
    def _():
        part_next.wait_send()


def finish_kernel(a, b, c, d, a_out, b_out, c_out, d_out, out_sem):
    stores = [
        pltpu.make_async_copy(source, target, out_sem.at[i])
        for i, (source, target) in enumerate(
            ((a, a_out), (b, b_out), (c, c_out), (d, d_out))
        )
    ]
    for store in stores:
        store.start()
    for store in stores:
        store.wait()


def finish(*arrays):
    return pl.pallas_call(
        finish_kernel,
        out_shape=[jax.ShapeDtypeStruct(a.shape, a.dtype) for a in arrays],
        in_specs=[pl.BlockSpec(memory_space=pltpu.VMEM)] * 4,
        out_specs=[pl.BlockSpec(memory_space=pltpu.MemorySpace.HBM)] * 4,
        scratch_shapes=[pltpu.SemaphoreType.DMA((4,))],
        compiler_params=pltpu.CompilerParams(vmem_limit_bytes=VMEM_BYTES),
        name="finish",
    )(*arrays)


def local(
    depth, flux_east, flux_south, river_section, bed_level, rough_class, manning_table, bank_cell
):
    rows, columns = depth.shape
    owned = river_section.shape[0]
    width, _ = bank_cell.shape
    ext = rows + 2 * HALO
    operands = [
        pltpu.with_memory_space_constraint(a, pltpu.MemorySpace.HBM)
        for a in (
            manning_table,
            depth,
            flux_east,
            flux_south,
            bed_level,
            rough_class,
            river_section.reshape(1, owned),
            bank_cell,
        )
    ]
    hbm = pl.BlockSpec(memory_space=pltpu.MemorySpace.HBM)
    vmem = pl.BlockSpec(memory_space=pltpu.VMEM)
    tile = pltpu.VMEM((rows, columns), jnp.float32)
    line = pltpu.VMEM((1, owned), jnp.float32)
    wide = pltpu.VMEM((ext, columns), jnp.float32)
    dma = pltpu.SemaphoreType.DMA
    depth, flux_east, flux_south, section = pl.pallas_call(
        flood_kernel,
        out_shape=[tile, tile, tile, line],
        in_specs=[hbm] * 8,
        out_specs=[vmem] * 4,
        scratch_shapes=[
            pltpu.SMEM(manning_table.shape, jnp.float32),
            pltpu.VMEM((4, rows, columns), jnp.float32),
            pltpu.VMEM((rows, columns), jnp.int32),
            pltpu.VMEM((4, 2 * HALO, columns), jnp.float32),
            pltpu.VMEM((2 * HALO, columns), jnp.int32),
        ]
        + [wide] * 13
        + [
            tile,
            pltpu.VMEM((5, 1, owned), jnp.float32),
            pltpu.VMEM((5, width, owned), jnp.int32),
            pltpu.VMEM((3, 1, owned), jnp.float32),
            line,
            line,
            dma((8,)),
            dma((2, 5)),
            dma((2, 5)),
            dma((2, 4)),
            dma((2, 4)),
            dma((2,)),
            dma((2,)),
        ],
        compiler_params=pltpu.CompilerParams(
            collective_id=0, has_side_effects=True, vmem_limit_bytes=VMEM_BYTES
        ),
        name="flood",
    )(*operands)
    depth, flux_east, flux_south, section = finish(depth, flux_east, flux_south, section)
    return depth, flux_east, flux_south, section.reshape(owned)


def solution(mesh):
    return jax.shard_map(
        local,
        mesh=mesh,
        in_specs=(
            P(("runs", "gy"), None),
            P(("runs", "gy"), None),
            P(("runs", "gy"), None),
            P(("runs", "gy")),
            P("gy", None),
            P("gy", None),
            P(),
            P(None, "gy"),
        ),
        out_specs=(
            P(("runs", "gy"), None),
            P(("runs", "gy"), None),
            P(("runs", "gy"), None),
            P(("runs", "gy")),
        ),
        check_vma=False,
    )
```

profile of v0, /device:TPU:1, one launch (start us, length us, event | category | flops | bytes accessed | tf_op | source)
XLA Modules:
  0.0 15.8 jit_solution(15366526356946053783)
XLA Ops:
  0.6 14.2 %flood.1 = (f32[32,1920]{1,0:T(8,128)S(1)}, f32[32,1920]{1,0:T(8,128)S(1)}, f32[32,1920]{1,0:T(8,128)S(1)}, f32[1,128]{1,0:T(1,128)S(1)}) custom-call(f32[8]{0:T(128)} %table_in.1, f32[32,1920]{1,0:T(8,128)} %depth_in.1, f32[32,1920]{1,0:T(8,128)} %east_in.1, f32[32,1920]{1,0:T(8,128)} %south_in.1, f32[32,1920]{1,0:T(8,128)} %bed_in.1, s32[32,1920]{1,0:T(8,128)} %rough_in.1, ...), custom_call_target="tpu_custom_call" | custom-call | tf_op jit(solution)/shard_map/flood/pallas_call | solution.py:631
  14.9 0.9 %finish.1 = (f32[32,1920]{1,0:T(8,128)}, f32[32,1920]{1,0:T(8,128)}, f32[32,1920]{1,0:T(8,128)}, f32[1,128]{1,0:T(1,128)}) custom-call(f32[32,1920]{1,0:T(8,128)S(1)} %get-tuple-element.12.a, f32[32,1920]{1,0:T(8,128)S(1)} %get-tuple-element.13.b, f32[32,1920]{1,0:T(8,128)S(1)} %get-tuple-element.14.c, f32[1,128]{1,0:T(1,128)S(1)} %get-tuple-element.15.d), custom_call_target="tpu_custom_call" | custom-call | tf_op jit(solution)/shard_map/finish/pallas_call | solution.py:594
where the time goes:
time: 15.9 us; the launch traced here: 15.8 us
  Pallas kernels  15.1 us (95%)
  between operations  0.64 us (4%)
    pallas_call x1, Pallas kernels, local(): pl.pallas_call(flood_kernel, out_shape=[tile, tile, tile, line], in_specs...  14.2 us
    pallas_call x1, Pallas kernels, finish(): pl.pallas_call(finish_kernel, out_shape=[jax.ShapeDtypeStruct(a.shape, a....  0.89 us

commit v1 on v0

--- a/solution.py
+++ b/solution.py
@@ -9,6 +9,7 @@
 
 STEPS = 4
 HALO = STEPS
+SOON = HALO - 1
 LANES = 128
 TILE = 8
 
@@ -74,6 +75,10 @@
     raw_rough,
     edge,
     edge_rough,
+    far,
+    far_rough,
+    tops,
+    bottoms,
     surf,
     fe,
     fs,
@@ -156,16 +161,27 @@
             send(section_in, sections.at[slot], node_ssem.at[0, i], node_rsem.at[0, i], offset),
             send(cells_in, cells.at[slot], node_ssem.at[1, i], node_rsem.at[1, i], offset),
         )
-    strip_sends = {}
+    strip_sends, far_sends = {}, {}
     for i, offset in enumerate((-1, 1)):
-        theirs = slice(0, HALO) if offset < 0 else slice(rows - HALO, rows)
-        lands = slice(0, HALO) if offset < 0 else slice(HALO, 2 * HALO)
-        sources = [field.at[theirs] for field in fields] + [rough_in.at[theirs]]
-        targets = [edge.at[j, lands] for j in range(4)] + [edge_rough.at[lands]]
-        strip_sends[offset] = [
-            send(source, target, strip_ssem.at[i, j], strip_rsem.at[i, j], offset)
-            for j, (source, target) in enumerate(zip(sources, targets))
-        ]
+        for group, (first, stop) in enumerate(((0, SOON), (SOON, HALO))):
+            if offset < 0:
+                theirs, lands = slice(first, stop), slice(first, stop)
+            else:
+                theirs = slice(rows - stop, rows - first)
+                lands = slice(2 * HALO - stop, 2 * HALO - first)
+            there_f, there_r = ((edge, edge_rough), (far, far_rough))[group]
+            sources = [field.at[theirs] for field in fields] + [rough_in.at[theirs]]
+            targets = [there_f.at[j, lands] for j in range(4)] + [there_r.at[lands]]
+            (strip_sends, far_sends)[group][offset] = [
+                send(
+                    source,
+                    target,
+                    strip_ssem.at[i, 5 * group + j],
+                    strip_rsem.at[i, 5 * group + j],
+                    offset,
+                )
+                for j, (source, target) in enumerate(zip(sources, targets))
+            ]
 
     pl.semaphore_wait(barrier, jnp.minimum(me, 2) + jnp.minimum(tiles - 1 - me, 2))
     for offset in OFFSETS:
@@ -174,11 +190,16 @@
             for copy in node_sends[offset]:
                 copy.start()
 
-    for offset in (-1, 1):
-        @pl.when(there(offset))
-        def _():
-            for copy in strip_sends[offset]:
-                copy.start()
+    for sends in (strip_sends, far_sends):
+        for offset in (-1, 1):
+            @pl.when(there(offset))
+            def _():
+                for copy in sends[offset]:
+                    copy.start()
+
+    later = slice(SOON, 2 * HALO - SOON)
+    edge[:, later, :] = jnp.zeros((4, 2 * (HALO - SOON), columns), jnp.float32)
+    edge_rough[later, :] = jnp.zeros((2 * (HALO - SOON), columns), jnp.int32)
 
     for load in loads:
         load.wait()
@@ -205,7 +226,7 @@
         return pltpu.roll(value, LANES - shift, 1)
 
     def lanes_to(value, preceding, shift):
-        mixed = jnp.where(lane_id >= LANES - shift, preceding, value)
+        mixed = jnp.where(lane_id < LANES - shift, value, preceding)
         return pltpu.roll(mixed, shift, 1)
 
     def south(value):
@@ -222,7 +243,7 @@
         return jnp.maximum(jnp.maximum(surf_a, surf_b) - bed_top, FLOOR * LEVEL)
 
     def power_log(flow_depth):
-        return jnp.log(flow_depth) * (-7.0 / 3.0)
+        return lax.log2(flow_depth) * (-7.0 / 3.0)
 
     def damping(flux, drag, power):
         return 1.0 / (1.0 + drag * jnp.abs(flux) * power)
@@ -259,6 +280,9 @@
     def got(name, c, count):
         return after.get((name, c), zeros(count))
 
+    def two_on(name, c, count):
+        return jnp.where(lane_id < LANES - 2, after[name, c], got(name, c + 1, count))
+
     inner = rows - TILE
 
     def own_chunk(c):
@@ -268,6 +292,7 @@
         mann[:rows, at(c)] = mine
         here = raw[0, :, at(c)] * LEVEL + floor
         surf[:rows, at(c)] = here
+        tops[0, :, at(c)] = here[:TILE]
         turned = [turn(a, 1) for a in (here, floor, mine)]
         put("own", c, (here, turned))
         yield
@@ -277,8 +302,7 @@
             jnp.where(lane_id < LANES - 1, a, b) for a, b in zip(turned, following[1])
         )
         pair = here + east
-        pair_next = following[0] + following[1][0]
-        mixed = turn(jnp.where(lane_id < 2, pair_next, pair), 2)
+        put("pair", c, turn(pair, 2))
         top = jnp.maximum(floor, floor_e)
         drag = square(mine + mann_e)
         max_e[:rows, at(c)] = top
@@ -293,11 +317,11 @@
         depth_s = depth_of(here[:inner], below_s, top)
         log_s = power_log(depth_s)
         yield
-        boxes[:rows, at(c)] = pair + mixed
-        power_e, power_s = jnp.exp(log_e), jnp.exp(log_s)
+        power_e, power_s = jnp.exp2(log_e), jnp.exp2(log_s)
         flux_e = raw[2, :, at(c)] * FLOW
         flux_s = raw[3, :inner, at(c)] * FLOW
         yield
+        boxes[:rows, at(c)] = pair + two_on("pair", c, rows)
         damp_e = damping(flux_e, drag, power_e)
         damp_s = damping(flux_s, drag_b, power_s)
         yield
@@ -310,72 +334,83 @@
         yield
         partial[:, at(c)] = here + (west - new_east)
 
-    wave(by(1, (own_chunk(c) for c in range(chunks))))
+    wave(by(2, (own_chunk(c) for c in range(chunks))))
     after.clear()
 
-    for offset in OFFSETS:
-        @pl.when(there(-offset))
-        def _():
-            for copy in node_sends[offset]:
-                copy.wait_recv()
-
-        @pl.when(absent(-offset))
-        def _():
-            sections[2 - offset] = jnp.zeros((1, owned), jnp.float32)
-            cells[2 - offset] = jnp.full((cells.shape[1], owned), FAR, jnp.int32)
-
-    section = jnp.concatenate([sections[i] for i in range(5)], axis=1)
-    cell = jnp.concatenate([cells[i, 0:1, :] for i in range(5)], axis=1)
-    local = cell - (me * rows - HALO) * columns
-    valid = (local >= 0) & (local < ext * columns)
-    local = jnp.where(valid, local, 0)
-    from_top = ((local.astype(jnp.float32) + 0.5) * (1.0 / columns)).astype(jnp.int32)
-    column = local - from_top * columns
-    chunk = column >> 7
-    lane = column & (LANES - 1)
-    own = valid & (from_top >= HALO) & (from_top < rows + HALO)
-    place = jnp.where(own, chunk * rows + from_top - HALO, -1)
-    near = slice(owned, 4 * owned)
-    beyond = jnp.where(from_top < HALO, from_top + HALO, from_top - rows - HALO)
-    place_edge = jnp.where(valid & jnp.logical_not(own), chunk * TILE + beyond, -1)
+    def nodes_of(offsets):
+        for offset in offsets:
+            @pl.when(there(-offset))
+            def _():
+                for copy in node_sends[offset]:
+                    copy.wait_recv()
+
+            @pl.when(absent(-offset))
+            def _():
+                sections[2 - offset] = jnp.zeros((1, owned), jnp.float32)
+                cells[2 - offset] = jnp.full((cells.shape[1], owned), FAR, jnp.int32)
 
     def one_hot(count, index):
-        hit = lax.broadcasted_iota(jnp.int32, (count, index.shape[1]), 0) == index
-        return jnp.where(hit, 1.0, 0.0).astype(jnp.bfloat16)
-
-    hit = one_hot(chunks * rows, place[:, near])
-    hit_edge = one_hot(-(-chunks * TILE // 16) * 16, place_edge)
-    lane_hit = lax.broadcasted_iota(jnp.int32, (LANES, total), 0) == lane
-    levels = section * (LEVEL * INTO)
-    level_high = levels.astype(jnp.bfloat16).astype(jnp.float32)
-    weights = jnp.concatenate(
-        [
-            jnp.where(lane_hit, value, 0.0)
-            for value in (level_high, levels - level_high, jnp.ones_like(levels))
-        ],
-        axis=0,
-    ).astype(jnp.bfloat16)
-    contract = (((1,), (1,)), ((), ()))
-    spread = lax.dot_general(
-        hit, weights[:, near], contract, preferred_element_type=jnp.float32
-    )
-    spread_edge = lax.dot_general(
-        hit_edge, weights, contract, preferred_element_type=jnp.float32
-    )
-    summed = counted = (zeros(ext),) * 2
-    for c in range(chunks):
-        block = jnp.concatenate(
+        found = lax.broadcasted_iota(jnp.int32, (count, index.shape[1]), 0) == index
+        return jnp.where(found, 1.0, 0.0).astype(jnp.bfloat16)
+
+    def locate(slots):
+        section = jnp.concatenate([sections[i] for i in slots], axis=1)
+        cell = jnp.concatenate([cells[i, 0:1, :] for i in slots], axis=1)
+        local = cell - (me * rows - HALO) * columns
+        valid = (local >= 0) & (local < ext * columns)
+        local = jnp.where(valid, local, 0)
+        from_top = ((local.astype(jnp.float32) + 0.5) * (1.0 / columns)).astype(jnp.int32)
+        column = local - from_top * columns
+        chunk = column >> 7
+        own = valid & (from_top >= HALO) & (from_top < rows + HALO)
+        place = jnp.where(own, chunk * rows + from_top - HALO, -1)
+        beyond = jnp.where(from_top < HALO, from_top + HALO, from_top - rows - HALO)
+        place_edge = jnp.where(valid & jnp.logical_not(own), chunk * TILE + beyond, -1)
+        lane = column & (LANES - 1)
+        lane_hit = lax.broadcasted_iota(jnp.int32, (LANES, lane.shape[1]), 0) == lane
+        levels = section * (LEVEL * INTO)
+        level_high = levels.astype(jnp.bfloat16).astype(jnp.float32)
+        weights = jnp.concatenate(
             [
-                spread[c * rows : (c + 1) * rows],
-                spread_edge[c * TILE : (c + 1) * TILE],
+                jnp.where(lane_hit, value, 0.0)
+                for value in (level_high, levels - level_high, jnp.ones_like(levels))
             ],
             axis=0,
-        )
+        ).astype(jnp.bfloat16)
+        return section, own, place, place_edge, lane_hit, weights
+
+    def spread_by(hits, weights):
+        return lax.dot_general(
+            hits, weights, (((1,), (1,)), ((), ())), preferred_element_type=jnp.float32
+        )
+
+    def planes(block):
         level = block[:, :LANES] + block[:, LANES : 2 * LANES]
-        tally[:, at(c)], summed = last_four(level, summed)
-        count = block[:, 2 * LANES :] * INTO
-        number4[:, at(c)], counted = last_four(count, counted)
-        number[:, at(c)] = count * GAIN
+        return level, block[:, 2 * LANES :] * INTO
+
+    def share(name, span, c, level, count):
+        count4, counted[name] = last_four(count, counted[name])
+        tally[span, at(c)] = level
+        number[span, at(c)] = count * GAIN
+        number4[span, at(c)] = count4
+
+    outer = slice(rows, ext)
+    counted = {"own": (zeros(rows),) * 2, "edge": (zeros(TILE),) * 2}
+    nodes_of((-1, 1))
+    section, own, place, place_edge, lane_hit, weights = locate((1, 2, 3))
+    hit = one_hot(chunks * rows, place)
+    spread = spread_by(hit, weights)
+    for c in range(chunks):
+        share("own", slice(0, rows), c, *planes(spread[c * rows : (c + 1) * rows]))
+
+    nodes_of((-2, 2))
+    _, _, _, place_more, _, weights_more = locate((0, 4))
+    hit_edge = one_hot(
+        -(-chunks * TILE // 16) * 16, jnp.concatenate([place_edge, place_more], axis=1)
+    )
+    spread = spread_by(hit_edge, jnp.concatenate([weights, weights_more], axis=1))
+    for c in range(chunks):
+        share("edge", outer, c, *planes(spread[c * TILE : (c + 1) * TILE]))
 
     for i, offset in enumerate((-1, 1)):
         @pl.when(there(-offset))
@@ -388,8 +423,6 @@
             lands = slice(HALO * i, HALO * (i + 1))
             edge[:, lands, :] = jnp.zeros((4, HALO, columns), jnp.float32)
             edge_rough[lands, :] = jnp.zeros((HALO, columns), jnp.int32)
-
-    outer = slice(rows, ext)
 
     def edge_chunk(c):
         floor = edge[1, :, at(c)] * LEVEL
@@ -404,8 +437,7 @@
             jnp.where(lane_id < LANES - 1, a, b) for a, b in zip(turned, following[1])
         )
         pair = here + east
-        pair_next = following[0] + following[1][0]
-        mixed = turn(jnp.where(lane_id < 2, pair_next, pair), 2)
+        put("edge_pair", c, turn(pair, 2))
         top = jnp.maximum(floor, floor_e)
         drag = square(mine + mann_e)
         max_e[outer, at(c)] = top
@@ -422,12 +454,17 @@
         drag_s[inner:, at(c)] = drag_b
         depth_s = depth_of(whole[inner:], below_s, top)
         log_s = power_log(depth_s)
-        yield
-        boxes[outer, at(c)] = pair + mixed
-        power_e, power_s = jnp.exp(log_e), jnp.exp(log_s)
+        levels = tally[:, at(c)]
+        put("edge_levels", c, levels)
+        spill = levels + lanes_to(levels, got("edge_levels", c - 1, ext), 1)
+        put("edge_spill", c, spill)
+        yield
+        spill2 = lanes_to(spill, got("edge_spill", c - 1, ext), 2)
+        power_e, power_s = jnp.exp2(log_e), jnp.exp2(log_s)
         flux_e = edge[2, :, at(c)] * FLOW
         flux_s = jnp.concatenate([raw[3, inner:, at(c)], edge[3, :, at(c)]], axis=0) * FLOW
         yield
+        boxes[outer, at(c)] = pair + two_on("edge_pair", c, TILE)
         damp_e = damping(flux_e, drag, power_e)
         damp_s = damping(flux_s, drag_b, power_s)
         yield
@@ -435,6 +472,7 @@
         new_south = closed_south((flux_s - depth_s * (below_s - whole[inner:])) * damp_s)
         fe[outer, at(c)] = new_east
         fs[inner:, at(c)] = new_south
+        bottoms[0, :, at(c)] = new_south[:TILE]
         put("edge_east", c, new_east)
         west = lanes_to(new_east, got("edge_east", c - 1, TILE), 1)
         new_south = jnp.concatenate([fs[:inner, at(c)], new_south], axis=0)
@@ -442,15 +480,22 @@
         surf[:, at(c)] = (
             jnp.concatenate([partial[:, at(c)], here + (west - new_east)], axis=0)
             + (north(new_south) - new_south)
-            + (tally[:, at(c)] - number4[:, at(c)] * whole)
-        )
+            + (spill + spill2 - number4[:, at(c)] * whole)
+        )
+
+    def spilled(name, c, moved):
+        count = moved.shape[0]
+        put((name, 1), c, moved)
+        once = moved + lanes_to(moved, got((name, 1), c - 1, count), 1)
+        put((name, 2), c, once)
+        return lambda: once + lanes_to(once, got((name, 2), c - 1, count), 2)
 
     def chunk_step(step, c):
-        last = step == STEPS - 1
-        count = rows if last else ext
+        count = rows if step == STEPS - 2 else ext
         span = slice(0, count)
         whole = surf[:, at(c)]
         here = whole[:count]
+        tops[step, :, at(c)] = whole[:TILE]
         turned = turn(here, 1)
         put(("here", step), c, (here, turned))
         yield
@@ -462,43 +507,152 @@
         below_s = south(whole)
         depth_s = depth_of(whole, below_s, max_s[:, at(c)])
         log_s = power_log(depth_s)
-        if not last:
-            pair = here + east
-            pair_next = following[0] + following[1]
-            mixed = turn(jnp.where(lane_id < 2, pair_next, pair), 2)
+        pair = here + east
+        put(("pair", step), c, turn(pair, 2))
         box = boxes[span, at(c)]
-        moved = number[span, at(c)] * box
-        put(("moved", step), c, moved)
-        spill = lanes_to(moved, got(("moved", step), c - 1, count), 1)
-        yield
-        power_e, power_s = jnp.exp(log_e), jnp.exp(log_s)
-        if not last:
-            boxes[:, at(c)] = KEEP * box + (pair + mixed)
-        spill = moved + spill
-        put(("spill", step), c, spill)
-        spill2 = lanes_to(spill, got(("spill", step), c - 1, count), 2)
-        yield
+        spill = spilled(("moved", step), c, number[span, at(c)] * box + KEEP**step * tally[span, at(c)])
+        yield
+        power_e, power_s = jnp.exp2(log_e), jnp.exp2(log_s)
+        source = spill()
+        yield
+        boxes[span, at(c)] = KEEP * box + (pair + two_on(("pair", step), c, count))
         flux_e, flux_s = fe[span, at(c)], fs[:, at(c)]
         damp_e = damping(flux_e, drag_e[span, at(c)], power_e)
         damp_s = damping(flux_s, drag_s[:, at(c)], power_s)
-        source = KEEP**step * tally[span, at(c)] + (spill + spill2) - number4[span, at(c)] * here
+        source = source - number4[span, at(c)] * here
         yield
         new_east = closed_east(c, (flux_e - depth_e * (east - here)) * damp_e)
         new_south = closed_south((flux_s - depth_s * (below_s - whole)) * damp_s)
         put(("east", step), c, new_east)
         west = lanes_to(new_east, got(("east", step), c - 1, count), 1)
-        if last:
-            east_out[:, at(c)] = new_east * (1.0 / FLOW)
-            south_out[:, at(c)] = new_south[:rows] * (1.0 / FLOW)
+        fe[span, at(c)] = new_east
+        fs[span, at(c)] = new_south[:count]
+        bottoms[step, :, at(c)] = new_south[inner:rows]
+        yield
+        level = here + (west - new_east) + (north(new_south) - new_south)[:count] + source
+        surf[span, at(c)] = level
+
+    def halo_step(step, c):
+        if step == 0:
+            floor = edge[1, :, at(c)] * LEVEL
+            here = edge[0, :, at(c)] * LEVEL + floor
+            mine = roughness(edge_rough[:, at(c)])
+            turned = [turn(a, 1) for a in (here, floor, mine)]
         else:
-            fe[:, at(c)] = new_east
-            fs[:, at(c)] = new_south
-        yield
-        level = here + (west - new_east) + (north(new_south) - new_south)[:count] + source
-        if last:
-            depth_out[:, at(c)] = level * (1.0 / LEVEL) - raw[1, :, at(c)]
+            here = surf[outer, at(c)]
+            turned = [turn(here, 1)]
+        put(("halo", step), c, turned)
+        yield
+        yield
+        following = after.get((("halo", step), c + 1), [zeros(TILE)] * 3)
+        nexts = [jnp.where(lane_id < LANES - 1, a, b) for a, b in zip(turned, following)]
+        east = nexts[0]
+        pair = here + east
+        put(("halo_pair", step), c, turn(pair, 2))
+
+        def southward(value, top):
+            return south(jnp.concatenate([value, top], axis=0))[:TILE]
+
+        below_s = southward(here, tops[step, :, at(c)])
+        if step == 0:
+            top = jnp.maximum(floor, nexts[1])
+            drag = square(mine + nexts[2])
+            top_s = jnp.maximum(floor, southward(floor, bed[:TILE, at(c)]))
+            drag_b = square(mine + southward(mine, mann[:TILE, at(c)]))
+            max_e[outer, at(c)] = top
+            drag_e[outer, at(c)] = drag
+            max_s[outer, at(c)] = top_s
+            drag_s[outer, at(c)] = drag_b
+            flux_e, flux_s = (edge[i, :, at(c)] * FLOW for i in (2, 3))
+            moved = tally[outer, at(c)]
         else:
-            surf[:, at(c)] = level
+            top, drag = max_e[outer, at(c)], drag_e[outer, at(c)]
+            top_s, drag_b = max_s[outer, at(c)], drag_s[outer, at(c)]
+            flux_e, flux_s = fe[outer, at(c)], fs[outer, at(c)]
+            box = boxes[outer, at(c)]
+            moved = number[outer, at(c)] * box + KEEP**step * tally[outer, at(c)]
+        depth_e = depth_of(here, east, top)
+        log_e = power_log(depth_e)
+        depth_s = depth_of(here, below_s, top_s)
+        log_s = power_log(depth_s)
+        spill = spilled(("halo_moved", step), c, moved)
+        yield
+        power_e, power_s = jnp.exp2(log_e), jnp.exp2(log_s)
+        source = spill()
+        yield
+        total = pair + two_on(("halo_pair", step), c, TILE)
+        boxes[outer, at(c)] = total if step == 0 else KEEP * box + total
+        damp_e = damping(flux_e, drag, power_e)
+        damp_s = damping(flux_s, drag_b, power_s)
+        source = source - number4[outer, at(c)] * here
+        yield
+        new_east = closed_east(c, (flux_e - depth_e * (east - here)) * damp_e)
+        new_south = (flux_s - depth_s * (below_s - here)) * damp_s
+        new_south = jnp.where(shut_first, 0.0, new_south)
+        put(("halo_east", step), c, new_east)
+        west = lanes_to(new_east, got(("halo_east", step), c - 1, TILE), 1)
+        fe[outer, at(c)] = new_east
+        fs[outer, at(c)] = new_south
+        yield
+        into = north(jnp.concatenate([bottoms[step, :, at(c)], new_south], axis=0))[TILE:]
+        surf[outer, at(c)] = here + (west - new_east) + (into - new_south) + source
+
+    def last_chunk(c):
+        step = STEPS - 1
+        here = surf[:rows, at(c)]
+        turned = turn(here, 1)
+        put("last", c, turned)
+        yield
+        yield
+        east = jnp.where(lane_id < LANES - 1, turned, got("last", c + 1, rows))
+        depth_e = depth_of(here, east, max_e[:rows, at(c)])
+        log_e = power_log(depth_e)
+        below_s = south(here)[:inner]
+        depth_s = depth_of(here[:inner], below_s, max_s[:inner, at(c)])
+        log_s = power_log(depth_s)
+        spill = spilled(
+            "last_moved",
+            c,
+            number[:rows, at(c)] * boxes[:rows, at(c)] + KEEP**step * tally[:rows, at(c)],
+        )
+        yield
+        power_e, power_s = jnp.exp2(log_e), jnp.exp2(log_s)
+        source = spill()
+        yield
+        flux_e, flux_s = fe[:rows, at(c)], fs[:inner, at(c)]
+        damp_e = damping(flux_e, drag_e[:rows, at(c)], power_e)
+        damp_s = damping(flux_s, drag_s[:inner, at(c)], power_s)
+        source = source - number4[:rows, at(c)] * here
+        yield
+        new_east = closed_east(c, (flux_e - depth_e * (east - here)) * damp_e)
+        new_south = (flux_s - depth_s * (below_s - here[:inner])) * damp_s
+        put("last_east", c, new_east)
+        west = lanes_to(new_east, got("last_east", c - 1, rows), 1)
+        east_out[:, at(c)] = new_east * (1.0 / FLOW)
+        south_out[:inner, at(c)] = new_south * (1.0 / FLOW)
+        fs[:inner, at(c)] = new_south
+        yield
+        partial[:, at(c)] = here + (west - new_east) + source
+
+    def last_edge(c):
+        whole = jnp.concatenate(
+            [surf[inner:, at(c)], surf[:TILE, at(c)]], axis=0
+        )
+        here = whole[: 2 * TILE]
+        below_s = south(whole)[: 2 * TILE]
+        depth_s = depth_of(here, below_s, max_s[inner:, at(c)])
+        log_s = power_log(depth_s)
+        yield
+        power_s = jnp.exp2(log_s)
+        flux_s = fs[inner:, at(c)]
+        yield
+        damp_s = damping(flux_s, drag_s[inner:, at(c)], power_s)
+        yield
+        new_south = closed_south((flux_s - depth_s * (below_s - here)) * damp_s)
+        south_out[inner:, at(c)] = new_south[:TILE] * (1.0 / FLOW)
+        new_south = jnp.concatenate([fs[:inner, at(c)], new_south], axis=0)
+        level = partial[:, at(c)] + (north(new_south) - new_south)[:rows]
+        depth_out[:, at(c)] = level * (1.0 / LEVEL) - raw[1, :, at(c)]
 
     flat = {}
 
@@ -510,23 +664,23 @@
         yield
         following = after.get(("node", c + 1), (zeros(rows), zeros(rows)))
         pair = here + jnp.where(lane_id < LANES - 1, turned, following[1])
-        pair_next = following[0] + following[1]
-        mixed = turn(jnp.where(lane_id < 2, pair_next, pair), 2)
-        yield
-        flat[c] = KEEP * boxes[:rows, at(c)] + (pair + mixed)
-
-    batches = by(3, (edge_chunk(c) for c in range(chunks))) + [[]]
+        put("node_pair", c, turn(pair, 2))
+        yield
+        yield
+        flat[c] = KEEP * boxes[:rows, at(c)] + (pair + two_on("node_pair", c, rows))
+
+    batches = by(5, (edge_chunk(c) for c in range(chunks))) + [[]] * 3
     for step in range(1, STEPS - 1):
-        batches += by(1, (chunk_step(step, c) for c in range(chunks)))
-    wave(batches + [[]] * 5 + by(3, (node_chunk(c) for c in range(chunks))))
+        batches += by(3, (chunk_step(step, c) for c in range(chunks))) + [[]]
+    wave(batches + [[]] * 2 + by(5, (node_chunk(c) for c in range(chunks))))
     flat = [flat[c] for c in range(chunks)]
 
     turned = jnp.concatenate(halves(jnp.concatenate(flat, axis=0).T), axis=0)
     picked = jnp.dot(turned, hit, preferred_element_type=jnp.float32)
     picked = picked[:LANES] + picked[LANES:]
-    picked = jnp.sum(jnp.where(lane_hit[:, near], picked, 0.0), axis=0, keepdims=True)
+    picked = jnp.sum(jnp.where(lane_hit, picked, 0.0), axis=0, keepdims=True)
     final = jnp.where(
-        own[:, near], KEEP**STEPS * section[:, near] + (GAIN / LEVEL) * picked, 0.0
+        own, KEEP**STEPS * section + (GAIN / LEVEL) * picked, 0.0
     )
     for i in range(3):
         part[i] = final[:, i * owned : (i + 1) * owned]
@@ -542,7 +696,23 @@
     def _():
         part_next.start()
 
-    wave(by(1, (chunk_step(STEPS - 1, c) for c in range(chunks))))
+    for i, offset in enumerate((-1, 1)):
+        @pl.when(there(-offset))
+        def _():
+            for copy in far_sends[offset]:
+                copy.wait_recv()
+
+            row = HALO - 1 + i
+            edge[:, row : row + 1, :] = far[:, row : row + 1, :]
+            edge_rough[row : row + 1, :] = far_rough[row : row + 1, :]
+
+    lasting = by(3, (last_chunk(c) for c in range(chunks)))
+    batches = []
+    for step in range(STEPS - 1):
+        batches += by(5, (halo_step(step, c) for c in range(chunks))) + [[]] * 4
+    for i, batch in enumerate(lasting):
+        batches[i + 3] = batches[i + 3] + batch
+    wave(batches + by(5, (last_edge(c) for c in range(chunks))))
 
     for offset in OFFSETS:
         @pl.when(there(offset))
@@ -553,7 +723,7 @@
     for offset in (-1, 1):
         @pl.when(there(offset))
         def _():
-            for copy in strip_sends[offset]:
+            for copy in strip_sends[offset] + far_sends[offset]:
                 copy.wait_send()
 
     section_out[...] = part[1]
@@ -639,6 +809,10 @@
             pltpu.VMEM((rows, columns), jnp.int32),
             pltpu.VMEM((4, 2 * HALO, columns), jnp.float32),
             pltpu.VMEM((2 * HALO, columns), jnp.int32),
+            pltpu.VMEM((4, 2 * HALO, columns), jnp.float32),
+            pltpu.VMEM((2 * HALO, columns), jnp.int32),
+            pltpu.VMEM((STEPS - 1, TILE, columns), jnp.float32),
+            pltpu.VMEM((STEPS - 1, TILE, columns), jnp.float32),
         ]
         + [wide] * 13
         + [
@@ -649,8 +823,8 @@
             line,
             line,
             dma((8,)),
-            dma((2, 5)),
-            dma((2, 5)),
+            dma((2, 10)),
+            dma((2, 10)),
             dma((2, 4)),
             dma((2, 4)),
             dma((2,)),

time: 15.9 us -> 13.8 us (0.87)
  Pallas kernels: 15.1 us -> 13 us
    pallas_call x1, Pallas kernels: 14.2 us -> 12.2 us  [local(): pl.pallas_call(flood_kernel, out_shape=[tile, tile, tile, line], in_specs...]
where the time goes in v1:
time: 13.8 us; the launch traced here: 13.7 us
  Pallas kernels  13 us (94%)
  between operations  0.64 us (5%)
    pallas_call x1, Pallas kernels, local(): pl.pallas_call(flood_kernel, out_shape=[tile, tile, tile, line], in_specs...  12.2 us
    pallas_call x1, Pallas kernels, finish(): pl.pallas_call(finish_kernel, out_shape=[jax.ShapeDtypeStruct(a.shape, a....  0.89 us

profile of v1, /device:TPU:1, one launch (start us, length us, event | category | flops | bytes accessed | tf_op | source)
XLA Modules:
  0.0 13.7 jit_solution(4437384015168765816)
XLA Ops:
  0.6 12.2 %flood.1 = (f32[32,1920]{1,0:T(8,128)S(1)}, f32[32,1920]{1,0:T(8,128)S(1)}, f32[32,1920]{1,0:T(8,128)S(1)}, f32[1,128]{1,0:T(1,128)S(1)}) custom-call(f32[8]{0:T(128)} %table_in.1, f32[32,1920]{1,0:T(8,128)} %depth_in.1, f32[32,1920]{1,0:T(8,128)} %east_in.1, f32[32,1920]{1,0:T(8,128)} %south_in.1, f32[32,1920]{1,0:T(8,128)} %bed_in.1, s32[32,1920]{1,0:T(8,128)} %rough_in.1, ...), custom_call_target="tpu_custom_call" | custom-call | tf_op jit(solution)/shard_map/flood/pallas_call | solution.py:801
  12.8 0.9 %finish.1 = (f32[32,1920]{1,0:T(8,128)}, f32[32,1920]{1,0:T(8,128)}, f32[32,1920]{1,0:T(8,128)}, f32[1,128]{1,0:T(1,128)}) custom-call(f32[32,1920]{1,0:T(8,128)S(1)} %get-tuple-element.12.a, f32[32,1920]{1,0:T(8,128)S(1)} %get-tuple-element.13.b, f32[32,1920]{1,0:T(8,128)S(1)} %get-tuple-element.14.c, f32[1,128]{1,0:T(1,128)S(1)} %get-tuple-element.15.d), custom_call_target="tpu_custom_call" | custom-call | tf_op jit(solution)/shard_map/finish/pallas_call | solution.py:764

commit v2 on v1

--- a/solution.py
+++ b/solution.py
@@ -9,7 +9,7 @@
 
 STEPS = 4
 HALO = STEPS
-SOON = HALO - 1
+TIERS = ((0, 2), (2, 3), (3, 4))
 LANES = 128
 TILE = 8
 
@@ -120,6 +120,8 @@
     def absent(offset):
         return jnp.logical_not(there(offset))
 
+    edge[...] = jnp.zeros(edge.shape, jnp.float32)
+    edge_rough[...] = jnp.zeros(edge_rough.shape, jnp.int32)
     barrier = pltpu.get_barrier_semaphore()
     for offset in OFFSETS:
         @pl.when(there(offset))
@@ -161,27 +163,34 @@
             send(section_in, sections.at[slot], node_ssem.at[0, i], node_rsem.at[0, i], offset),
             send(cells_in, cells.at[slot], node_ssem.at[1, i], node_rsem.at[1, i], offset),
         )
-    strip_sends, far_sends = {}, {}
+    def span_of(tier, field, offset):
+        first, stop = TIERS[tier]
+        if field == 2 or (field == 3 and offset < 0):
+            return max(first - 1, 0), stop - 1
+        return first, stop
+
+    def landing(tier, field, offset):
+        first, stop = span_of(tier, field, offset)
+        return slice(first, stop) if offset < 0 else slice(2 * HALO - stop, 2 * HALO - first)
+
+    strip_sends = {}
     for i, offset in enumerate((-1, 1)):
-        for group, (first, stop) in enumerate(((0, SOON), (SOON, HALO))):
-            if offset < 0:
-                theirs, lands = slice(first, stop), slice(first, stop)
-            else:
-                theirs = slice(rows - stop, rows - first)
-                lands = slice(2 * HALO - stop, 2 * HALO - first)
-            there_f, there_r = ((edge, edge_rough), (far, far_rough))[group]
-            sources = [field.at[theirs] for field in fields] + [rough_in.at[theirs]]
-            targets = [there_f.at[j, lands] for j in range(4)] + [there_r.at[lands]]
-            (strip_sends, far_sends)[group][offset] = [
-                send(
-                    source,
-                    target,
-                    strip_ssem.at[i, 5 * group + j],
-                    strip_rsem.at[i, 5 * group + j],
-                    offset,
+        for tier in range(len(TIERS)):
+            strip_sends[tier, offset] = []
+            for j in range(5):
+                first, stop = span_of(tier, j, offset)
+                theirs = slice(first, stop) if offset < 0 else slice(rows - stop, rows - first)
+                lands = landing(tier, j, offset)
+                if j < 4:
+                    source = fields[j].at[theirs]
+                    target = edge.at[j, lands] if tier == 0 else far.at[tier - 1, j, lands]
+                else:
+                    source = rough_in.at[theirs]
+                    target = edge_rough.at[lands] if tier == 0 else far_rough.at[tier - 1, lands]
+                sem = 5 * tier + j
+                strip_sends[tier, offset].append(
+                    send(source, target, strip_ssem.at[i, sem], strip_rsem.at[i, sem], offset)
                 )
-                for j, (source, target) in enumerate(zip(sources, targets))
-            ]
 
     pl.semaphore_wait(barrier, jnp.minimum(me, 2) + jnp.minimum(tiles - 1 - me, 2))
     for offset in OFFSETS:
@@ -190,16 +199,12 @@
             for copy in node_sends[offset]:
                 copy.start()
 
-    for sends in (strip_sends, far_sends):
+    for tier in range(len(TIERS)):
         for offset in (-1, 1):
             @pl.when(there(offset))
             def _():
-                for copy in sends[offset]:
+                for copy in strip_sends[tier, offset]:
                     copy.start()
-
-    later = slice(SOON, 2 * HALO - SOON)
-    edge[:, later, :] = jnp.zeros((4, 2 * (HALO - SOON), columns), jnp.float32)
-    edge_rough[later, :] = jnp.zeros((2 * (HALO - SOON), columns), jnp.int32)
 
     for load in loads:
         load.wait()
@@ -403,26 +408,11 @@
     for c in range(chunks):
         share("own", slice(0, rows), c, *planes(spread[c * rows : (c + 1) * rows]))
 
-    nodes_of((-2, 2))
-    _, _, _, place_more, _, weights_more = locate((0, 4))
-    hit_edge = one_hot(
-        -(-chunks * TILE // 16) * 16, jnp.concatenate([place_edge, place_more], axis=1)
-    )
-    spread = spread_by(hit_edge, jnp.concatenate([weights, weights_more], axis=1))
-    for c in range(chunks):
-        share("edge", outer, c, *planes(spread[c * TILE : (c + 1) * TILE]))
-
-    for i, offset in enumerate((-1, 1)):
+    for offset in (-1, 1):
         @pl.when(there(-offset))
         def _():
-            for copy in strip_sends[offset]:
+            for copy in strip_sends[0, offset]:
                 copy.wait_recv()
-
-        @pl.when(absent(-offset))
-        def _():
-            lands = slice(HALO * i, HALO * (i + 1))
-            edge[:, lands, :] = jnp.zeros((4, HALO, columns), jnp.float32)
-            edge_rough[lands, :] = jnp.zeros((HALO, columns), jnp.int32)
 
     def edge_chunk(c):
         floor = edge[1, :, at(c)] * LEVEL
@@ -436,8 +426,6 @@
         east, floor_e, mann_e = (
             jnp.where(lane_id < LANES - 1, a, b) for a, b in zip(turned, following[1])
         )
-        pair = here + east
-        put("edge_pair", c, turn(pair, 2))
         top = jnp.maximum(floor, floor_e)
         drag = square(mine + mann_e)
         max_e[outer, at(c)] = top
@@ -454,17 +442,16 @@
         drag_s[inner:, at(c)] = drag_b
         depth_s = depth_of(whole[inner:], below_s, top)
         log_s = power_log(depth_s)
-        levels = tally[:, at(c)]
+        levels = tally[:rows, at(c)]
         put("edge_levels", c, levels)
-        spill = levels + lanes_to(levels, got("edge_levels", c - 1, ext), 1)
+        spill = levels + lanes_to(levels, got("edge_levels", c - 1, rows), 1)
         put("edge_spill", c, spill)
         yield
-        spill2 = lanes_to(spill, got("edge_spill", c - 1, ext), 2)
+        spill2 = lanes_to(spill, got("edge_spill", c - 1, rows), 2)
         power_e, power_s = jnp.exp2(log_e), jnp.exp2(log_s)
         flux_e = edge[2, :, at(c)] * FLOW
         flux_s = jnp.concatenate([raw[3, inner:, at(c)], edge[3, :, at(c)]], axis=0) * FLOW
         yield
-        boxes[outer, at(c)] = pair + two_on("edge_pair", c, TILE)
         damp_e = damping(flux_e, drag, power_e)
         damp_s = damping(flux_s, drag_b, power_s)
         yield
@@ -477,11 +464,21 @@
         west = lanes_to(new_east, got("edge_east", c - 1, TILE), 1)
         new_south = jnp.concatenate([fs[:inner, at(c)], new_south], axis=0)
         yield
-        surf[:, at(c)] = (
-            jnp.concatenate([partial[:, at(c)], here + (west - new_east)], axis=0)
-            + (north(new_south) - new_south)
-            + (spill + spill2 - number4[:, at(c)] * whole)
-        )
+        gain_s = north(new_south) - new_south
+        surf[:rows, at(c)] = (
+            partial[:, at(c)]
+            + gain_s[:rows]
+            + (spill + spill2 - number4[:rows, at(c)] * whole[:rows])
+        )
+        surf[outer, at(c)] = here + (west - new_east) + gain_s[rows:]
+
+    def edge_source(c):
+        spill = spilled("edge_moved", c, tally[outer, at(c)])
+        yield
+        source = spill()
+        yield
+        here = (edge[0, :, at(c)] + edge[1, :, at(c)]) * LEVEL
+        surf[outer, at(c)] = surf[outer, at(c)] + (source - number4[outer, at(c)] * here)
 
     def spilled(name, c, moved):
         count = moved.shape[0]
@@ -491,7 +488,7 @@
         return lambda: once + lanes_to(once, got((name, 2), c - 1, count), 2)
 
     def chunk_step(step, c):
-        count = rows if step == STEPS - 2 else ext
+        count = rows
         span = slice(0, count)
         whole = surf[:, at(c)]
         here = whole[:count]
@@ -597,28 +594,35 @@
         into = north(jnp.concatenate([bottoms[step, :, at(c)], new_south], axis=0))[TILE:]
         surf[outer, at(c)] = here + (west - new_east) + (into - new_south) + source
 
-    def last_chunk(c):
-        step = STEPS - 1
+    def part_chunk(step, c):
+        last = step == STEPS - 1
         here = surf[:rows, at(c)]
         turned = turn(here, 1)
-        put("last", c, turned)
-        yield
-        yield
-        east = jnp.where(lane_id < LANES - 1, turned, got("last", c + 1, rows))
+        put(("here", step), c, (here, turned))
+        if not last:
+            tops[step, :, at(c)] = here[:TILE]
+        yield
+        yield
+        following = after.get((("here", step), c + 1), (zeros(rows), zeros(rows)))
+        east = jnp.where(lane_id < LANES - 1, turned, following[1])
         depth_e = depth_of(here, east, max_e[:rows, at(c)])
         log_e = power_log(depth_e)
         below_s = south(here)[:inner]
         depth_s = depth_of(here[:inner], below_s, max_s[:inner, at(c)])
         log_s = power_log(depth_s)
+        if not last:
+            pair = here + east
+            put(("pair", step), c, turn(pair, 2))
+        box = boxes[:rows, at(c)]
         spill = spilled(
-            "last_moved",
-            c,
-            number[:rows, at(c)] * boxes[:rows, at(c)] + KEEP**step * tally[:rows, at(c)],
+            ("moved", step), c, number[:rows, at(c)] * box + KEEP**step * tally[:rows, at(c)]
         )
         yield
         power_e, power_s = jnp.exp2(log_e), jnp.exp2(log_s)
         source = spill()
         yield
+        if not last:
+            boxes[:rows, at(c)] = KEEP * box + (pair + two_on(("pair", step), c, rows))
         flux_e, flux_s = fe[:rows, at(c)], fs[:inner, at(c)]
         damp_e = damping(flux_e, drag_e[:rows, at(c)], power_e)
         damp_s = damping(flux_s, drag_s[:inner, at(c)], power_s)
@@ -626,18 +630,20 @@
         yield
         new_east = closed_east(c, (flux_e - depth_e * (east - here)) * damp_e)
         new_south = (flux_s - depth_s * (below_s - here[:inner])) * damp_s
-        put("last_east", c, new_east)
-        west = lanes_to(new_east, got("last_east", c - 1, rows), 1)
-        east_out[:, at(c)] = new_east * (1.0 / FLOW)
-        south_out[:inner, at(c)] = new_south * (1.0 / FLOW)
+        put(("east", step), c, new_east)
+        west = lanes_to(new_east, got(("east", step), c - 1, rows), 1)
         fs[:inner, at(c)] = new_south
+        if last:
+            east_out[:, at(c)] = new_east * (1.0 / FLOW)
+            south_out[:inner, at(c)] = new_south * (1.0 / FLOW)
+        else:
+            fe[:rows, at(c)] = new_east
         yield
         partial[:, at(c)] = here + (west - new_east) + source
 
-    def last_edge(c):
-        whole = jnp.concatenate(
-            [surf[inner:, at(c)], surf[:TILE, at(c)]], axis=0
-        )
+    def join_chunk(step, c):
+        last = step == STEPS - 1
+        whole = jnp.concatenate([surf[inner:, at(c)], surf[:TILE, at(c)]], axis=0)
         here = whole[: 2 * TILE]
         below_s = south(whole)[: 2 * TILE]
         depth_s = depth_of(here, below_s, max_s[inner:, at(c)])
@@ -649,10 +655,38 @@
         damp_s = damping(flux_s, drag_s[inner:, at(c)], power_s)
         yield
         new_south = closed_south((flux_s - depth_s * (below_s - here)) * damp_s)
-        south_out[inner:, at(c)] = new_south[:TILE] * (1.0 / FLOW)
+        if last:
+            south_out[inner:, at(c)] = new_south[:TILE] * (1.0 / FLOW)
+        else:
+            fs[inner:rows, at(c)] = new_south[:TILE]
+            bottoms[step, :, at(c)] = new_south[:TILE]
         new_south = jnp.concatenate([fs[:inner, at(c)], new_south], axis=0)
         level = partial[:, at(c)] + (north(new_south) - new_south)[:rows]
-        depth_out[:, at(c)] = level * (1.0 / LEVEL) - raw[1, :, at(c)]
+        if last:
+            depth_out[:, at(c)] = level * (1.0 / LEVEL) - raw[1, :, at(c)]
+        else:
+            surf[:rows, at(c)] = level
+
+    def arrive(tier):
+        for offset in (-1, 1):
+            @pl.when(there(-offset))
+            def _():
+                for copy in strip_sends[tier, offset]:
+                    copy.wait_recv()
+
+                for j in range(4):
+                    lands = landing(tier, j, offset)
+                    edge[j, lands, :] = far[tier - 1, j, lands, :]
+                lands = landing(tier, 4, offset)
+                edge_rough[lands, :] = far_rough[tier - 1, lands, :]
+
+    def again(steps, step, extra):
+        batches = []
+        for done in range(steps):
+            batches += by(5, (halo_step(done, c) for c in range(chunks))) + [[]] * 4
+        for i, batch in enumerate(by(3, (part_chunk(step, c) for c in range(chunks)))):
+            batches[i + 3] = batches[i + 3] + batch
+        wave(batches + by(5, (join_chunk(step, c) for c in range(chunks))) + extra)
 
     flat = {}
 
@@ -669,10 +703,20 @@
         yield
         flat[c] = KEEP * boxes[:rows, at(c)] + (pair + two_on("node_pair", c, rows))
 
-    batches = by(5, (edge_chunk(c) for c in range(chunks))) + [[]] * 3
-    for step in range(1, STEPS - 1):
-        batches += by(3, (chunk_step(step, c) for c in range(chunks))) + [[]]
-    wave(batches + [[]] * 2 + by(5, (node_chunk(c) for c in range(chunks))))
+    wave(by(5, (edge_chunk(c) for c in range(chunks))))
+
+    nodes_of((-2, 2))
+    _, _, _, place_more, _, weights_more = locate((0, 4))
+    hit_edge = one_hot(
+        -(-chunks * TILE // 16) * 16, jnp.concatenate([place_edge, place_more], axis=1)
+    )
+    spread = spread_by(hit_edge, jnp.concatenate([weights, weights_more], axis=1))
+    for c in range(chunks):
+        share("edge", outer, c, *planes(spread[c * TILE : (c + 1) * TILE]))
+    wave(by(5, (edge_source(c) for c in range(chunks))) + [[]] + by(3, (chunk_step(1, c) for c in range(chunks))))
+
+    arrive(1)
+    again(2, 2, by(5, (node_chunk(c) for c in range(chunks))))
     flat = [flat[c] for c in range(chunks)]
 
     turned = jnp.concatenate(halves(jnp.concatenate(flat, axis=0).T), axis=0)
@@ -696,23 +740,8 @@
     def _():
         part_next.start()
 
-    for i, offset in enumerate((-1, 1)):
-        @pl.when(there(-offset))
-        def _():
-            for copy in far_sends[offset]:
-                copy.wait_recv()
-
-            row = HALO - 1 + i
-            edge[:, row : row + 1, :] = far[:, row : row + 1, :]
-            edge_rough[row : row + 1, :] = far_rough[row : row + 1, :]
-
-    lasting = by(3, (last_chunk(c) for c in range(chunks)))
-    batches = []
-    for step in range(STEPS - 1):
-        batches += by(5, (halo_step(step, c) for c in range(chunks))) + [[]] * 4
-    for i, batch in enumerate(lasting):
-        batches[i + 3] = batches[i + 3] + batch
-    wave(batches + by(5, (last_edge(c) for c in range(chunks))))
+    arrive(2)
+    again(3, 3, [])
 
     for offset in OFFSETS:
         @pl.when(there(offset))
@@ -723,8 +752,9 @@
     for offset in (-1, 1):
         @pl.when(there(offset))
         def _():
-            for copy in strip_sends[offset] + far_sends[offset]:
-                copy.wait_send()
+            for tier in range(len(TIERS)):
+                for copy in strip_sends[tier, offset]:
+                    copy.wait_send()
 
     section_out[...] = part[1]
 
@@ -809,8 +839,8 @@
             pltpu.VMEM((rows, columns), jnp.int32),
             pltpu.VMEM((4, 2 * HALO, columns), jnp.float32),
             pltpu.VMEM((2 * HALO, columns), jnp.int32),
-            pltpu.VMEM((4, 2 * HALO, columns), jnp.float32),
-            pltpu.VMEM((2 * HALO, columns), jnp.int32),
+            pltpu.VMEM((len(TIERS) - 1, 4, 2 * HALO, columns), jnp.float32),
+            pltpu.VMEM((len(TIERS) - 1, 2 * HALO, columns), jnp.int32),
             pltpu.VMEM((STEPS - 1, TILE, columns), jnp.float32),
             pltpu.VMEM((STEPS - 1, TILE, columns), jnp.float32),
         ]
@@ -823,8 +853,8 @@
             line,
             line,
             dma((8,)),
-            dma((2, 10)),
-            dma((2, 10)),
+            dma((2, 15)),
+            dma((2, 15)),
             dma((2, 4)),
             dma((2, 4)),
             dma((2,)),

time: 13.8 us -> 13.6 us (0.986)
  Pallas kernels: 13 us -> 12.8 us
    pallas_call x1, Pallas kernels: 12.2 us -> 11.9 us  [local(): pl.pallas_call(flood_kernel, out_shape=[tile, tile, tile, line], in_specs...]
where the time goes in v2:
time: 13.6 us; the launch traced here: 13.5 us
  Pallas kernels  12.8 us (94%)
  between operations  0.64 us (5%)
    pallas_call x1, Pallas kernels, local(): pl.pallas_call(flood_kernel, out_shape=[tile, tile, tile, line], in_specs...  11.9 us
    pallas_call x1, Pallas kernels, finish(): pl.pallas_call(finish_kernel, out_shape=[jax.ShapeDtypeStruct(a.shape, a....  0.89 us

profile of v2, /device:TPU:1, one launch (start us, length us, event | category | flops | bytes accessed | tf_op | source)
XLA Modules:
  0.0 13.5 jit_solution(16616585055772144797)
XLA Ops:
  0.6 11.9 %flood.1 = (f32[32,1920]{1,0:T(8,128)S(1)}, f32[32,1920]{1,0:T(8,128)S(1)}, f32[32,1920]{1,0:T(8,128)S(1)}, f32[1,128]{1,0:T(1,128)S(1)}) custom-call(f32[8]{0:T(128)} %table_in.1, f32[32,1920]{1,0:T(8,128)} %depth_in.1, f32[32,1920]{1,0:T(8,128)} %east_in.1, f32[32,1920]{1,0:T(8,128)} %south_in.1, f32[32,1920]{1,0:T(8,128)} %bed_in.1, s32[32,1920]{1,0:T(8,128)} %rough_in.1, ...), custom_call_target="tpu_custom_call" | custom-call | tf_op jit(solution)/shard_map/flood/pallas_call | solution.py:831
  12.6 0.9 %finish.1 = (f32[32,1920]{1,0:T(8,128)}, f32[32,1920]{1,0:T(8,128)}, f32[32,1920]{1,0:T(8,128)}, f32[1,128]{1,0:T(1,128)}) custom-call(f32[32,1920]{1,0:T(8,128)S(1)} %get-tuple-element.12.a, f32[32,1920]{1,0:T(8,128)S(1)} %get-tuple-element.13.b, f32[32,1920]{1,0:T(8,128)S(1)} %get-tuple-element.14.c, f32[1,128]{1,0:T(1,128)S(1)} %get-tuple-element.15.d), custom_call_target="tpu_custom_call" | custom-call | tf_op jit(solution)/shard_map/finish/pallas_call | solution.py:794

commit v3 on v2

--- a/solution.py
+++ b/solution.py
@@ -401,12 +401,21 @@
 
     outer = slice(rows, ext)
     counted = {"own": (zeros(rows),) * 2, "edge": (zeros(TILE),) * 2}
+    section_m, own_m, place, place_m, lane_m, weights_m = locate((2,))
+    hit_m = one_hot(chunks * rows, place)
+    spread = spread_by(hit_m, weights_m)
+    for c in range(chunks):
+        level, count = planes(spread[c * rows : (c + 1) * rows])
+        tally[:rows, at(c)] = level
+        number[:rows, at(c)] = count
     nodes_of((-1, 1))
-    section, own, place, place_edge, lane_hit, weights = locate((1, 2, 3))
-    hit = one_hot(chunks * rows, place)
-    spread = spread_by(hit, weights)
+    section_n, own_n, place, place_n, lane_n, weights_n = locate((1, 3))
+    hit_n = one_hot(chunks * rows, place)
+    spread = spread_by(hit_n, weights_n)
     for c in range(chunks):
-        share("own", slice(0, rows), c, *planes(spread[c * rows : (c + 1) * rows]))
+        level, count = planes(spread[c * rows : (c + 1) * rows])
+        level = level + tally[:rows, at(c)]
+        share("own", slice(0, rows), c, level, count + number[:rows, at(c)])
 
     for offset in (-1, 1):
         @pl.when(there(-offset))
@@ -684,7 +693,7 @@
         batches = []
         for done in range(steps):
             batches += by(5, (halo_step(done, c) for c in range(chunks))) + [[]] * 4
-        for i, batch in enumerate(by(3, (part_chunk(step, c) for c in range(chunks)))):
+        for i, batch in enumerate(by(5, (part_chunk(step, c) for c in range(chunks)))):
             batches[i + 3] = batches[i + 3] + batch
         wave(batches + by(5, (join_chunk(step, c) for c in range(chunks))) + extra)
 
@@ -703,31 +712,33 @@
         yield
         flat[c] = KEEP * boxes[:rows, at(c)] + (pair + two_on("node_pair", c, rows))
 
-    wave(by(5, (edge_chunk(c) for c in range(chunks))))
+    wave(by(15, (edge_chunk(c) for c in range(chunks))))
 
     nodes_of((-2, 2))
-    _, _, _, place_more, _, weights_more = locate((0, 4))
+    _, _, _, place_f, _, weights_f = locate((0, 4))
     hit_edge = one_hot(
-        -(-chunks * TILE // 16) * 16, jnp.concatenate([place_edge, place_more], axis=1)
+        -(-chunks * TILE // 16) * 16, jnp.concatenate([place_m, place_n, place_f], axis=1)
     )
-    spread = spread_by(hit_edge, jnp.concatenate([weights, weights_more], axis=1))
+    spread = spread_by(hit_edge, jnp.concatenate([weights_m, weights_n, weights_f], axis=1))
     for c in range(chunks):
         share("edge", outer, c, *planes(spread[c * TILE : (c + 1) * TILE]))
-    wave(by(5, (edge_source(c) for c in range(chunks))) + [[]] + by(3, (chunk_step(1, c) for c in range(chunks))))
+    wave(by(5, (edge_source(c) for c in range(chunks))) + [[]] + by(4, (chunk_step(1, c) for c in range(chunks))))
 
     arrive(1)
     again(2, 2, by(5, (node_chunk(c) for c in range(chunks))))
     flat = [flat[c] for c in range(chunks)]
 
     turned = jnp.concatenate(halves(jnp.concatenate(flat, axis=0).T), axis=0)
-    picked = jnp.dot(turned, hit, preferred_element_type=jnp.float32)
-    picked = picked[:LANES] + picked[LANES:]
-    picked = jnp.sum(jnp.where(lane_hit, picked, 0.0), axis=0, keepdims=True)
-    final = jnp.where(
-        own, KEEP**STEPS * section + (GAIN / LEVEL) * picked, 0.0
-    )
-    for i in range(3):
-        part[i] = final[:, i * owned : (i + 1) * owned]
+
+    def levels_of(section, own, hit, lane_hit):
+        picked = jnp.dot(turned, hit, preferred_element_type=jnp.float32)
+        picked = picked[:LANES] + picked[LANES:]
+        picked = jnp.sum(jnp.where(lane_hit, picked, 0.0), axis=0, keepdims=True)
+        return jnp.where(own, KEEP**STEPS * section + (GAIN / LEVEL) * picked, 0.0)
+
+    final = levels_of(section_n, own_n, hit_n, lane_n)
+    part[0] = final[:, :owned]
+    part[2] = final[:, owned:]
 
     part_prev = send(part.at[0], high, part_ssem.at[0], part_rsem.at[0], -1)
     part_next = send(part.at[2], low, part_ssem.at[1], part_rsem.at[1], 1)
@@ -739,6 +750,8 @@
     @pl.when(there(1))
     def _():
         part_next.start()
+
+    part[1] = levels_of(section_m, own_m, hit_m, lane_m)
 
     arrive(2)
     again(3, 3, [])

time: 13.6 us -> 13.5 us (level)
  no operation moved by 1% of the time
where the time goes in v3:
time: 13.5 us; the launch traced here: 13.4 us
  Pallas kernels  12.7 us (94%)
  between operations  0.64 us (5%)
    pallas_call x1, Pallas kernels, local(): pl.pallas_call(flood_kernel, out_shape=[tile, tile, tile, line], in_specs...  11.8 us
    pallas_call x1, Pallas kernels, finish(): pl.pallas_call(finish_kernel, out_shape=[jax.ShapeDtypeStruct(a.shape, a....  0.89 us

profile of v3, /device:TPU:1, one launch (start us, length us, event | category | flops | bytes accessed | tf_op | source)
XLA Modules:
  0.0 13.4 jit_solution(16647170219396131613)
XLA Ops:
  0.6 11.8 %flood.1 = (f32[32,1920]{1,0:T(8,128)S(1)}, f32[32,1920]{1,0:T(8,128)S(1)}, f32[32,1920]{1,0:T(8,128)S(1)}, f32[1,128]{1,0:T(1,128)S(1)}) custom-call(f32[8]{0:T(128)} %table_in.1, f32[32,1920]{1,0:T(8,128)} %depth_in.1, f32[32,1920]{1,0:T(8,128)} %east_in.1, f32[32,1920]{1,0:T(8,128)} %south_in.1, f32[32,1920]{1,0:T(8,128)} %bed_in.1, s32[32,1920]{1,0:T(8,128)} %rough_in.1, ...), custom_call_target="tpu_custom_call" | custom-call | tf_op jit(solution)/shard_map/flood/pallas_call | solution.py:844
  12.5 0.9 %finish.1 = (f32[32,1920]{1,0:T(8,128)}, f32[32,1920]{1,0:T(8,128)}, f32[32,1920]{1,0:T(8,128)}, f32[1,128]{1,0:T(1,128)}) custom-call(f32[32,1920]{1,0:T(8,128)S(1)} %get-tuple-element.12.a, f32[32,1920]{1,0:T(8,128)S(1)} %get-tuple-element.13.b, f32[32,1920]{1,0:T(8,128)S(1)} %get-tuple-element.14.c, f32[1,128]{1,0:T(1,128)S(1)} %get-tuple-element.15.d), custom_call_target="tpu_custom_call" | custom-call | tf_op jit(solution)/shard_map/finish/pallas_call | solution.py:807

commit v4 on v3

--- a/solution.py
+++ b/solution.py
@@ -417,6 +417,16 @@
         level = level + tally[:rows, at(c)]
         share("own", slice(0, rows), c, level, count + number[:rows, at(c)])
 
+    blocks = -(-chunks * TILE // 16) * 16
+    spread = spread_by(
+        one_hot(blocks, jnp.concatenate([place_m, place_n], axis=1)),
+        jnp.concatenate([weights_m, weights_n], axis=1),
+    )
+    for c in range(chunks):
+        level, count = planes(spread[c * TILE : (c + 1) * TILE])
+        tally[outer, at(c)] = level
+        number[outer, at(c)] = count
+
     for offset in (-1, 1):
         @pl.when(there(-offset))
         def _():
@@ -495,48 +505,6 @@
         once = moved + lanes_to(moved, got((name, 1), c - 1, count), 1)
         put((name, 2), c, once)
         return lambda: once + lanes_to(once, got((name, 2), c - 1, count), 2)
-
-    def chunk_step(step, c):
-        count = rows
-        span = slice(0, count)
-        whole = surf[:, at(c)]
-        here = whole[:count]
-        tops[step, :, at(c)] = whole[:TILE]
-        turned = turn(here, 1)
-        put(("here", step), c, (here, turned))
-        yield
-        yield
-        following = after.get((("here", step), c + 1), (zeros(count), zeros(count)))
-        east = jnp.where(lane_id < LANES - 1, turned, following[1])
-        depth_e = depth_of(here, east, max_e[span, at(c)])
-        log_e = power_log(depth_e)
-        below_s = south(whole)
-        depth_s = depth_of(whole, below_s, max_s[:, at(c)])
-        log_s = power_log(depth_s)
-        pair = here + east
-        put(("pair", step), c, turn(pair, 2))
-        box = boxes[span, at(c)]
-        spill = spilled(("moved", step), c, number[span, at(c)] * box + KEEP**step * tally[span, at(c)])
-        yield
-        power_e, power_s = jnp.exp2(log_e), jnp.exp2(log_s)
-        source = spill()
-        yield
-        boxes[span, at(c)] = KEEP * box + (pair + two_on(("pair", step), c, count))
-        flux_e, flux_s = fe[span, at(c)], fs[:, at(c)]
-        damp_e = damping(flux_e, drag_e[span, at(c)], power_e)
-        damp_s = damping(flux_s, drag_s[:, at(c)], power_s)
-        source = source - number4[span, at(c)] * here
-        yield
-        new_east = closed_east(c, (flux_e - depth_e * (east - here)) * damp_e)
-        new_south = closed_south((flux_s - depth_s * (below_s - whole)) * damp_s)
-        put(("east", step), c, new_east)
-        west = lanes_to(new_east, got(("east", step), c - 1, count), 1)
-        fe[span, at(c)] = new_east
-        fs[span, at(c)] = new_south[:count]
-        bottoms[step, :, at(c)] = new_south[inner:rows]
-        yield
-        level = here + (west - new_east) + (north(new_south) - new_south)[:count] + source
-        surf[span, at(c)] = level
 
     def halo_step(step, c):
         if step == 0:
@@ -712,17 +680,24 @@
         yield
         flat[c] = KEEP * boxes[:rows, at(c)] + (pair + two_on("node_pair", c, rows))
 
-    wave(by(15, (edge_chunk(c) for c in range(chunks))))
+    wave(
+        by(15, (edge_chunk(c) for c in range(chunks)))
+        + [[]] * 5
+        + by(5, (part_chunk(1, c) for c in range(chunks)))
+    )
 
     nodes_of((-2, 2))
     _, _, _, place_f, _, weights_f = locate((0, 4))
-    hit_edge = one_hot(
-        -(-chunks * TILE // 16) * 16, jnp.concatenate([place_m, place_n, place_f], axis=1)
+    spread = spread_by(one_hot(blocks, place_f), weights_f)
+    for c in range(chunks):
+        level, count = planes(spread[c * TILE : (c + 1) * TILE])
+        level = level + tally[outer, at(c)]
+        share("edge", outer, c, level, count + number[outer, at(c)])
+    wave(
+        by(15, (edge_source(c) for c in range(chunks)))
+        + [[]]
+        + by(5, (join_chunk(1, c) for c in range(chunks)))
     )
-    spread = spread_by(hit_edge, jnp.concatenate([weights_m, weights_n, weights_f], axis=1))
-    for c in range(chunks):
-        share("edge", outer, c, *planes(spread[c * TILE : (c + 1) * TILE]))
-    wave(by(5, (edge_source(c) for c in range(chunks))) + [[]] + by(4, (chunk_step(1, c) for c in range(chunks))))
 
     arrive(1)
     again(2, 2, by(5, (node_chunk(c) for c in range(chunks))))

time: 13.5 us -> 13.4 us (level)
  the two profiles are of different devices: /device:TPU:1 before, /device:TPU:23 now
where the time goes in v4:
time: 13.4 us; the launch traced here: 13.2 us
  Pallas kernels  12.6 us (94%)
  between operations  0.64 us (5%)
    pallas_call x1, Pallas kernels, local(): pl.pallas_call(flood_kernel, out_shape=[tile, tile, tile, line], in_specs...  11.7 us
    pallas_call x1, Pallas kernels, finish(): pl.pallas_call(finish_kernel, out_shape=[jax.ShapeDtypeStruct(a.shape, a....  0.89 us

profile of v4, /device:TPU:23, one launch (start us, length us, event | category | flops | bytes accessed | tf_op | source)
XLA Modules:
  0.0 13.2 jit_solution(17540087078192801187)
XLA Ops:
  0.6 11.7 %flood.1 = (f32[32,1920]{1,0:T(8,128)S(1)}, f32[32,1920]{1,0:T(8,128)S(1)}, f32[32,1920]{1,0:T(8,128)S(1)}, f32[1,128]{1,0:T(1,128)S(1)}) custom-call(f32[8]{0:T(128)} %table_in.1, f32[32,1920]{1,0:T(8,128)} %depth_in.1, f32[32,1920]{1,0:T(8,128)} %east_in.1, f32[32,1920]{1,0:T(8,128)} %south_in.1, f32[32,1920]{1,0:T(8,128)} %bed_in.1, s32[32,1920]{1,0:T(8,128)} %rough_in.1, ...), custom_call_target="tpu_custom_call" | custom-call | tf_op jit(solution)/shard_map/flood/pallas_call | solution.py:819
  12.3 0.9 %finish.1 = (f32[32,1920]{1,0:T(8,128)}, f32[32,1920]{1,0:T(8,128)}, f32[32,1920]{1,0:T(8,128)}, f32[1,128]{1,0:T(1,128)}) custom-call(f32[32,1920]{1,0:T(8,128)S(1)} %get-tuple-element.12.a, f32[32,1920]{1,0:T(8,128)S(1)} %get-tuple-element.13.b, f32[32,1920]{1,0:T(8,128)S(1)} %get-tuple-element.14.c, f32[1,128]{1,0:T(1,128)S(1)} %get-tuple-element.15.d), custom_call_target="tpu_custom_call" | custom-call | tf_op jit(solution)/shard_map/finish/pallas_call | solution.py:782

commit v5 on v4

--- a/solution.py
+++ b/solution.py
@@ -199,12 +199,15 @@
             for copy in node_sends[offset]:
                 copy.start()
 
-    for tier in range(len(TIERS)):
+    def launch(*tiers_now):
         for offset in (-1, 1):
             @pl.when(there(offset))
             def _():
-                for copy in strip_sends[tier, offset]:
-                    copy.start()
+                for tier in tiers_now:
+                    for copy in strip_sends[tier, offset]:
+                        copy.start()
+
+    launch(0)
 
     for load in loads:
         load.wait()
@@ -341,6 +344,8 @@
 
     wave(by(2, (own_chunk(c) for c in range(chunks))))
     after.clear()
+
+    launch(1, 2)
 
     def nodes_of(offsets):
         for offset in offsets:

time: 13.4 us -> 13.4 us (level)
  the two profiles are of different devices: /device:TPU:23 before, /device:TPU:7 now
where the time goes in v5:
time: 13.4 us; the launch traced here: 13.2 us
  Pallas kernels  12.6 us (94%)
  between operations  0.64 us (5%)
    pallas_call x1, Pallas kernels, local(): pl.pallas_call(flood_kernel, out_shape=[tile, tile, tile, line], in_specs...  11.7 us
    pallas_call x1, Pallas kernels, finish(): pl.pallas_call(finish_kernel, out_shape=[jax.ShapeDtypeStruct(a.shape, a....  0.89 us

profile of v5, /device:TPU:7, one launch (start us, length us, event | category | flops | bytes accessed | tf_op | source)
XLA Modules:
  0.0 13.2 jit_solution(3251887780362683937)
XLA Ops:
  0.6 11.7 %flood.1 = (f32[32,1920]{1,0:T(8,128)S(1)}, f32[32,1920]{1,0:T(8,128)S(1)}, f32[32,1920]{1,0:T(8,128)S(1)}, f32[1,128]{1,0:T(1,128)S(1)}) custom-call(f32[8]{0:T(128)} %table_in.1, f32[32,1920]{1,0:T(8,128)} %depth_in.1, f32[32,1920]{1,0:T(8,128)} %east_in.1, f32[32,1920]{1,0:T(8,128)} %south_in.1, f32[32,1920]{1,0:T(8,128)} %bed_in.1, s32[32,1920]{1,0:T(8,128)} %rough_in.1, ...), custom_call_target="tpu_custom_call" | custom-call | tf_op jit(solution)/shard_map/flood/pallas_call | solution.py:824
  12.3 0.9 %finish.1 = (f32[32,1920]{1,0:T(8,128)}, f32[32,1920]{1,0:T(8,128)}, f32[32,1920]{1,0:T(8,128)}, f32[1,128]{1,0:T(1,128)}) custom-call(f32[32,1920]{1,0:T(8,128)S(1)} %get-tuple-element.12.a, f32[32,1920]{1,0:T(8,128)S(1)} %get-tuple-element.13.b, f32[32,1920]{1,0:T(8,128)S(1)} %get-tuple-element.14.c, f32[1,128]{1,0:T(1,128)S(1)} %get-tuple-element.15.d), custom_call_target="tpu_custom_call" | custom-call | tf_op jit(solution)/shard_map/finish/pallas_call | solution.py:787
